TPU v7x, 256 devices: a whole 4x4x8 slice. The times are simulated.
256 devices in a mesh: dp: 32 (over x, y, core), fsdp: 8 (over z).
Axes of the slice: x: 4, y: 4, z: 8, core: 2. Of those that a mesh axis runs over, the one named last changes fastest.
Arguments:
- frames: bfloat16 [131072, 1536], P(('dp', 'fsdp')), may hold values from -6 to 6
- segments: int32 [131072], replicated, may hold values from 0 to 383, never falling along the last dimension, each value on 1 to 750 neighbouring positions
- norm_gain: float32 [1536], replicated, may hold values from 0.1 to 1.9
- norm_bias: float32 [1536], replicated, may hold values from -3 to 3
- expand_weight: bfloat16 [1536, 3072], P('fsdp', 'dp'), may hold values from -0.15625 to 0.15625
- conv_kernel: float32 [31, 1536], replicated, may hold values from -1 to 1
- batch_scale: float32 [1536], replicated, may hold values from 0.1 to 1.9
- batch_shift: float32 [1536], replicated, may hold values from -3 to 3
- project_weight: bfloat16 [1536, 1536], P('fsdp', 'dp'), may hold values from -0.15625 to 0.15625
Outputs:
- output: bfloat16 [131072, 1536], P(('dp', 'fsdp'))
Inputs may be any that keep to these rules, and one draw needn't show every extreme that they name: `segments`: utterance numbers never fall along the frames; each utterance is 1 to 750 frames, and one has exactly 750.
All inputs are finite; a program needn't handle non-finite values.
Results may differ from a plain program's by a relative error of at most 0.0041.
Values may be sent and summed in bfloat16 or wider, within the bound.
A program may use at most 64 MiB of HBM per device.

v0:
```python
import jax
import jax.numpy as jnp
from jax import lax
from jax.sharding import PartitionSpec as P

EPSILON = 1e-05


def with_halo(cells, sides, width):
    for axis, dim in sides:
        count = lax.axis_size(axis)
        ends = count - 1
        head = lax.slice_in_dim(cells, 0, width, axis=dim)
        tail = lax.slice_in_dim(cells, cells.shape[dim] - width, cells.shape[dim], axis=dim)
        cells = jnp.concatenate(
            [
                lax.ppermute(tail, axis, [(i, (i + 1) % count) for i in range(ends)]),
                cells,
                lax.ppermute(head, axis, [((i + 1) % count, i) for i in range(ends)]),
            ],
            axis=dim,
        )
    return cells


def layer_norm(source, norm_gain, norm_bias):
    values = source.astype(jnp.float32)
    average = jnp.mean(values, axis=-1, keepdims=True)
    centered = values - average
    variance = jnp.mean(centered * centered, axis=-1, keepdims=True)
    return (centered * lax.rsqrt(variance + EPSILON) * norm_gain + norm_bias).astype(jnp.bfloat16)


def gated_units(expanded):
    channels = expanded.shape[1] // 2
    return (expanded[:, :channels] * jax.nn.sigmoid(expanded[:, channels:])).astype(jnp.bfloat16)


def depthwise(gated_ext, segment_ext, conv_kernel, row_count):
    half_span = conv_kernel.shape[0] // 2
    center = segment_ext[half_span : half_span + row_count]
    summed = jnp.zeros((row_count, gated_ext.shape[1]), jnp.float32)
    for offset in range(conv_kernel.shape[0]):
        same_utterance = (segment_ext[offset : offset + row_count] == center).astype(jnp.float32)
        shifted = gated_ext[offset : offset + row_count].astype(jnp.float32)
        summed = summed + conv_kernel[offset] * (shifted * same_utterance[:, None])
    return summed


def expand_gated(source, norm_gain, norm_bias, expand_weight):
    normed = layer_norm(source, norm_gain, norm_bias)
    tall_slice = lax.all_gather(expand_weight, "fsdp", axis=0, tiled=True)
    expanded = jnp.dot(
        normed,
        lax.all_gather(tall_slice, "dp", axis=1, tiled=True),
        preferred_element_type=jnp.float32,
    )
    return gated_units(expanded)


def project_out(activated, project_weight):
    tall_slice = lax.all_gather(project_weight, "fsdp", axis=0, tiled=True)
    return jnp.dot(
        activated,
        lax.all_gather(tall_slice, "dp", axis=1, tiled=True),
        preferred_element_type=jnp.float32,
    )


def local(
    frames,
    segments,
    norm_gain,
    norm_bias,
    expand_weight,
    conv_kernel,
    batch_scale,
    batch_shift,
    project_weight,
):
    row_count = frames.shape[0]
    half_span = conv_kernel.shape[0] // 2
    block_index = lax.axis_index(("dp", "fsdp"))
    segment_pad = jnp.pad(segments, (half_span, half_span), constant_values=-1)
    first_row = block_index * row_count
    segment_ext = lax.dynamic_slice_in_dim(segment_pad, first_row, row_count + 2 * half_span, 0)
    gated = expand_gated(frames, norm_gain, norm_bias, expand_weight)
    gated_ext = with_halo(gated, ((("dp", "fsdp"), 0),), half_span)
    summed = depthwise(gated_ext, segment_ext, conv_kernel, row_count)
    hidden = summed * batch_scale + batch_shift
    activated = (hidden * jax.nn.sigmoid(hidden)).astype(jnp.bfloat16)
    product = project_out(activated, project_weight)
    return (product + frames.astype(jnp.float32)).astype(jnp.bfloat16)


def solution(mesh):
    in_specs = (
        P(("dp", "fsdp"), None),
        P(),
        P(),
        P(),
        P("fsdp", "dp"),
        P(),
        P(),
        P(),
        P("fsdp", "dp"),
    )
    out_specs = P(("dp", "fsdp"), None)
    return jax.shard_map(local, mesh=mesh, in_specs=in_specs, out_specs=out_specs, check_vma=False)
```

profile of v0, /device:TPU:1, one launch (start us, length us, event | category | flops | bytes accessed | tf_op | source)
XLA Modules:
  0.0 197.1 jit_solution(15813584955124237646)
XLA Ops:
  6.5 0.0 copy-start.1
  6.5 0.0 copy-start
  6.5 0.0 all-gather.4.cloned.1.call-start
  6.5 23.9 %all_gather.12 = bf16[1536,96]{1,0:T(8,128)(2,1)S(1)} all-gather(bf16[192,96]{1,0:T(8,128)(2,1)} %param.13), channel_id=1, replica_groups=mesh['dp'=32,'fsdp'=8] {'fsdp'}, dimensions={0}, use_global_device_ids=true | all-gather | bytes 331776 | tf_op jit(solution)/shard_map/all_gather | solution.py:52
  30.4 0.0 copy-start.2
  30.4 0.0 copy-start.3
  30.4 0.9 copy.13
  31.3 0.0 all-gather.4.cloned.1.call-update
  31.3 0.0 all-gather.6.cloned.1.call-start
  31.4 18.6 %all-gather = bf16[8,192,48]{1,2,0:T(8,128)(2,1)S(1)} all-gather(bf16[1,192,48]{1,2,0:T(8,128)(2,1)} %bitcast.6), channel_id=1, replica_groups=mesh['dp'=32,'fsdp'=8] {'fsdp'}, dimensions={0}, use_global_device_ids=true | all-gather | bytes 165888 | tf_op jit(solution)/shard_map/all_gather | solution.py:62
  50.0 0.1 copy.14
  50.0 0.8 reshape.47
  50.9 0.0 all-gather.6.cloned.1.call-update
  50.9 0.8 pad_dynamic-slice_fusion
  51.7 0.0 copy-done.1
  51.7 0.9 slice_reduce_fusion.30
  52.6 0.0 copy-done
  52.6 0.3 convert_reduce_fusion
  52.9 0.6 fusion.2
  53.5 0.7 fusion.49
  54.1 0.7 fusion.46
  54.8 0.7 fusion.47
  55.5 0.7 fusion.48
  56.2 41.4 %all-gather.4.cloned.1.call-done = bf16[1536,3072]{0,1:T(8,128)(2,1)} async-done(((bf16[1536,96]{0,1:T(8,128)(2,1)}), bf16[1536,3072]{0,1:T(8,128)(2,1)}) %all-gather.4.cloned.1.call-update) | async-done | bytes 9437200 | tf_op jit(solution)/shard_map/all_gather | solution.py:55
  97.6 0.0 copy-done.2
  97.6 0.0 copy-done.3
  97.6 7.7 %fusion.12 = f32[512,3072]{1,0:T(8,128)S(1)} fusion(bf16[1536,3072]{0,1:T(8,128)(2,1)} %all-gather.4.cloned.1.call-done, bf16[512,1536]{1,0:T(8,128)(2,1)S(1)} %copy-done, f32[1536]{0:T(1024)S(1)} %copy-done.2, f32[1536]{0:T(1024)S(1)} %copy-done.3, f32[512]{0:T(512)S(1)} %add_rsqrt_fusion, f32[512]{0:T(512)S(1)} %broadcast_multiply_fusion), kind=kOutput, calls=%fused_computation.45 | convolution fusion | flops 4836556800 | bytes 17317888 | tf_op jit(solution)/shard_map/dot_general | solution.py:53
  105.3 0.8 fusion.10
  106.2 3.2 %collective-permute-start = (bf16[15,1536]{1,0:T(8,128)(2,1)S(1)}, bf16[15,1536]{1,0:T(8,128)(2,1)}, u32[]{:S(2)}, u32[]{:S(2)}) collective-permute-start(bf16[15,1536]{1,0:T(8,128)(2,1)S(1)} %get-tuple-element.36), channel_id=1, source_target_pairs={{0,1},{1,2},{2,3},{3,4},{4,5},{5,6},{6,7},{7,8},{8,9},{9,10},{10,1... | collective-permute-start | bytes 138248 | tf_op jit(solution)/shard_map/ppermute | solution.py:17
  109.4 3.8 %collective-permute-start.1 = (bf16[15,1536]{1,0:T(8,128)(2,1)S(1)}, bf16[15,1536]{1,0:T(8,128)(2,1)}, u32[]{:S(2)}, u32[]{:S(2)}) collective-permute-start(bf16[15,1536]{1,0:T(8,128)(2,1)S(1)} %get-tuple-element.37), channel_id=1, source_target_pairs={{1,0},{2,1},{3,2},{4,3},{5,4},{6,5},{7,6},{8,7},{9,8},{10,9},{11,1... | collective-permute-start | bytes 138248 | tf_op jit(solution)/shard_map/ppermute | solution.py:19
  113.2 0.8 slice_reduce_fusion.29
  114.0 37.7 %all-gather.6.cloned.1.call-done = bf16[1536,1536]{0,1:T(8,128)(2,1)} async-done(((bf16[1536,48]{0,1:T(8,128)(2,1)}), bf16[1536,1536]{0,1:T(8,128)(2,1)}) %all-gather.6.cloned.1.call-update) | async-done | bytes 4718608 | tf_op jit(solution)/shard_map/all_gather | solution.py:65
  151.7 0.0 collective-permute-done
  151.7 0.0 collective-permute-done.1
  151.7 38.5 %fusion.11 = bf16[512,1536]{1,0:T(8,128)(2,1)} fusion(bf16[512,1536]{1,0:T(8,128)(2,1)S(1)} %copy-done, bf16[1536,1536]{0,1:T(8,128)(2,1)} %all-gather.6.cloned.1.call-done, bf16[512,1536]{1,0:T(8,128)(2,1)S(1)} %fusion.10, bf16[15,1536]{1,0:T(8,128)(2,1)} %collective-permute-done.1, bf16[15,1536]{1,0:T(8,128)(2,1)} %collective-permute-done, ...), kind=kOutput, calls=%fused_computation.44 | convolution fusion | flops 2590507008 | bytes 9793536 | tf_op jit(solution)/shard_map/dot_general | solution.py:63
  (3 shorter events, 0.0 us)
Async XLA Ops:
  6.5 45.2 %copy-start.1 = (f32[31,1536]{1,0:T(8,128)S(1)}, f32[31,1536]{1,0:T(8,128)}, u32[]{:S(2)}) copy-start(f32[31,1536]{1,0:T(8,128)} %param.14) | copy-start | bytes 571396
  6.5 46.1 %copy-start = (bf16[512,1536]{1,0:T(8,128)(2,1)S(1)}, bf16[512,1536]{1,0:T(8,128)(2,1)}, u32[]{:S(2)}) copy-start(bf16[512,1536]{1,0:T(8,128)(2,1)} %param.9) | copy-start | bytes 4718596
  6.5 91.1 %all-gather.4.cloned.1.call-start = ((), (), s32[]{:S(2)}) async-start(), calls=%async_computation | async-start | bytes 9732096 | tf_op jit(solution)/shard_map/all_gather | solution.py:55
  30.4 67.2 %copy-start.2 = (f32[1536]{0:T(1024)S(1)}, f32[1536]{0:T(1024)}, u32[]{:S(2)}) copy-start(f32[1536]{0:T(1024)} %param.12) | copy-start | bytes 18436
  30.4 67.2 %copy-start.3 = (f32[1536]{0:T(1024)S(1)}, f32[1536]{0:T(1024)}, u32[]{:S(2)}) copy-start(f32[1536]{0:T(1024)} %param.11) | copy-start | bytes 18436
  31.3 120.4 %all-gather.6.cloned.1.call-start = ((), (), s32[]{:S(2)}) async-start(), calls=%async_computation.1 | async-start | bytes 4866048 | tf_op jit(solution)/shard_map/all_gather | solution.py:65
  106.2 45.5 %collective-permute-start = (bf16[15,1536]{1,0:T(8,128)(2,1)S(1)}, bf16[15,1536]{1,0:T(8,128)(2,1)}, u32[]{:S(2)}, u32[]{:S(2)}) collective-permute-start(bf16[15,1536]{1,0:T(8,128)(2,1)S(1)} %get-tuple-element.36), channel_id=1, source_target_pairs={{0,1},{1,2},{2,3},{3,4},{4,5},{5,6},{6,7},{7,8},{8,9},{9,10},{10,1... | collective-permute-start | bytes 138248 | tf_op jit(solution)/shard_map/ppermute | solution.py:17
  109.4 42.3 %collective-permute-start.1 = (bf16[15,1536]{1,0:T(8,128)(2,1)S(1)}, bf16[15,1536]{1,0:T(8,128)(2,1)}, u32[]{:S(2)}, u32[]{:S(2)}) collective-permute-start(bf16[15,1536]{1,0:T(8,128)(2,1)S(1)} %get-tuple-element.37), channel_id=1, source_target_pairs={{1,0},{2,1},{3,2},{4,3},{5,4},{6,5},{7,6},{8,7},{9,8},{10,9},{11,1... | collective-permute-start | bytes 138248 | tf_op jit(solution)/shard_map/ppermute | solution.py:19
Sparse Core Ops, SparseCore 0:
  31.5 66.1 all-gather.3
  100.2 51.4 all-gather.5
where the time goes:
time: 197 us
  waiting for transfers between devices  79.2 us (40%)
  matrix products  46.2 us (23%)
  blocking collectives  42.5 us (22%)
  between operations  13.5 us (7%)
  starting transfers between devices  7.04 us (4%)
  other arithmetic  4.45 us (2%)
  local copies, waits for them, and re-layouts  4.3 us (2%)
    all_gather x1, waiting for transfers between devices, expand_gated(): lax.all_gather(tall_slice, 'dp', axis=1, tiled=True)  41.4 us
    dot_general x1, matrix products, project_out(): jnp.dot(activated, lax.all_gather(tall_slice, 'dp', axis=1, tiled=True),...  38.5 us
    all_gather x1, waiting for transfers between devices, project_out(): lax.all_gather(tall_slice, 'dp', axis=1, tiled=True)  37.7 us
    all_gather x1, blocking collectives, expand_gated(): tall_slice = lax.all_gather(expand_weight, 'fsdp', axis=0, tiled=True)  23.9 us
    all_gather x1, blocking collectives, project_out(): tall_slice = lax.all_gather(project_weight, 'fsdp', axis=0, tiled=True)  18.6 us
    dot_general x1, matrix products, expand_gated(): jnp.dot(normed, lax.all_gather(tall_slice, 'dp', axis=1, tiled=True), pre...  7.67 us
  transfers between devices with their start and end apart: 4, of which 2 were waited for; matrix products, arithmetic and copies ran while one was open for 8% of the time, Pallas kernels for 0%

commit v1 on v0

v1 whole, which is shorter than its diff:
```python
import functools

import jax
import jax.numpy as jnp
from jax import lax
from jax.experimental import pallas as pl
from jax.experimental.pallas import tpu as pltpu
from jax.sharding import PartitionSpec as P

EPSILON = 1e-05
MESH = pl.DeviceIdType.MESH
F32 = jnp.float32
BF16 = jnp.bfloat16

NX, NY, NZ = 4, 4, 8
ROWS = 512
EDGE = 16
ALL = ROWS + 2 * EDGE
D = 1536
HALF = 15
TAPS = 31
SEMS = 256


def sigmoid(v):
    return 0.5 * jnp.tanh(0.5 * v) + 0.5


def kernel(
    frames, segs, gain, bias, w1, taps, scale, shift, w2, out,
    weights, rows, normed, active, result, gated, seg_raw, seg_col, before, after,
    own1, own2, own2r, parts1, parts2, gain_v, bias_v, taps_v, scale_v, shift_v,
    local_sem, send_sem, recv_sem,
):
    dp = lax.axis_index("dp")
    z = lax.axis_index("fsdp")
    x = dp // 8
    y = (dp // 2) % 4
    c = dp % 2
    s = 1 - 2 * c
    block = dp * 8 + z

    def dev(px, py, pz, pc):
        return (px * 8 + py * 2 + pc, pz)

    def xo(k):
        return (x + k + 2 * NX) % NX

    def yo(k):
        return (y + k + 2 * NY) % NY

    def zo(k):
        return (z + k + 2 * NZ) % NZ

    nxt = (block + 1) % 256
    prv = (block + 255) % 256
    next_dev = (nxt // 8, nxt % 8)
    prev_dev = (prv // 8, prv % 8)
    sibling = dev(x, y, z, 1 - c)
    x_dev = dev(xo(s), y, z, c)
    y_dev = dev(x, yo(s), z, c)
    z_dev = dev(x, y, zo(s), c)

    tile0 = block // 2
    seg_tiles = [
        jnp.maximum(tile0 - 1, 0),
        tile0,
        jnp.minimum(tile0 + 1, 127),
    ]
    loads = [
        pltpu.make_async_copy(w1, own1, local_sem.at[0]),
        pltpu.make_async_copy(w2, own2, local_sem.at[1]),
        pltpu.make_async_copy(frames, rows.at[pl.ds(EDGE, ROWS)], local_sem.at[2]),
        pltpu.make_async_copy(gain, gain_v, local_sem.at[3]),
        pltpu.make_async_copy(bias, bias_v, local_sem.at[4]),
        pltpu.make_async_copy(taps, taps_v, local_sem.at[5]),
        pltpu.make_async_copy(scale, scale_v, local_sem.at[6]),
        pltpu.make_async_copy(shift, shift_v, local_sem.at[7]),
    ] + [
        pltpu.make_async_copy(
            segs.at[pl.ds(pl.multiple_of(t * 8, 8), 8)],
            seg_raw.at[pl.ds(8 * i, 8)],
            local_sem.at[8 + i],
        )
        for i, t in enumerate(seg_tiles)
    ]
    for load in loads:
        load.start()

    barrier = pltpu.get_barrier_semaphore()
    peers = [
        dev(x, yo(dy), z, (c + dc) % 2) for dy in range(NY) for dc in range(2) if dy + dc
    ]
    peers += [dev(x, y, zo(k), c) for k in range(1, NZ)]
    peers += [dev(xo(k), y, z, c) for k in range(1, NX)]
    peers += [next_dev, prev_dev]
    for peer in peers:
        pl.semaphore_signal(barrier, inc=1, device_id=peer, device_id_type=MESH)
    pl.semaphore_wait(barrier, len(peers))

    count = [0]
    sent = []

    def post(src, dst, device, when=None):
        i = count[0]
        count[0] += 1
        copy = pltpu.make_async_remote_copy(
            src_ref=src, dst_ref=dst, send_sem=send_sem.at[i], recv_sem=recv_sem.at[i],
            device_id=device, device_id_type=MESH,
        )
        if when is None:
            copy.start()
            sent.append((copy, None))
        else:
            pl.when(when)(copy.start)
            sent.append((copy, when))
        return copy

    def send(ref, device, when=None):
        return post(ref, ref, device, when)

    loads[0].wait()
    loads[1].wait()
    own2r[...] = jnp.transpose(own2[...].astype(F32)).astype(BF16)
    mine = y * 2 + c
    spread = []
    for dy in (1, 3, 2, 0):
        for dc in range(2):
            first = pl.multiple_of(yo(dy) * 48, 16)
            if dy + dc == 0:
                keep = [
                    pltpu.make_async_copy(own1.at[pl.ds(first, 48)], parts1.at[mine], local_sem.at[11]),
                    pltpu.make_async_copy(own2r.at[pl.ds(first, 48)], parts2.at[mine], local_sem.at[12]),
                ]
                for copy in keep:
                    copy.start()
            else:
                to = dev(x, yo(dy), z, (c + dc) % 2)
                spread.append(post(own1.at[pl.ds(first, 48)], parts1.at[mine], to))
                spread.append(post(own2r.at[pl.ds(first, 48)], parts2.at[mine], to))

    loads[2].wait()
    halo = [
        post(rows.at[pl.ds(EDGE, EDGE)], rows.at[pl.ds(EDGE + ROWS, EDGE)], prev_dev),
        post(rows.at[pl.ds(ROWS, EDGE)], rows.at[pl.ds(0, EDGE)], next_dev),
    ]

    for copy in keep:
        copy.wait()
    for copy in spread:
        copy.wait_recv()
    full1 = jnp.concatenate([parts1[i].astype(F32) for i in range(8)], axis=1).astype(BF16)
    full2 = jnp.concatenate([parts2[i].astype(F32) for i in range(8)], axis=1).astype(BF16)
    for third in range(3):
        for p in range(2):
            j = 128 * (3 * p + third)
            weights[third, p, x, z, y] = full1[:, j : j + 128]
        weights[third, 2, x, z, y] = full2[:, 128 * third : 128 * third + 128]

    first_c = send(weights.at[2, :, x, z, y], x_dev)
    far_c = send(weights.at[2, :, x, z, y], dev(xo(2), y, z, c), c == 0)
    near = [
        send(weights.at[third, :, x, z, y], dev(x, y, zo(s * k), c))
        for k in (1, 2, 3)
        for third in (0, 1)
    ]
    far = send(weights.at[c, :, x, z, y], dev(x, y, zo(4), c))

    loads[3].wait()
    loads[4].wait()

    gain_row = jnp.concatenate([gain_v[i : i + 1, :] for i in range(12)], axis=1)
    bias_row = jnp.concatenate([bias_v[i : i + 1, :] for i in range(12)], axis=1)

    def norm(r0, n):
        v = rows[pl.ds(r0, n), :].astype(F32)
        mean = jnp.sum(v, axis=1, keepdims=True) * (1.0 / D)
        v = v - mean
        var = jnp.sum(v * v, axis=1, keepdims=True) * (1.0 / D)
        normed[pl.ds(r0, n), :] = (
            v * lax.rsqrt(var + EPSILON) * gain_row + bias_row
        ).astype(BF16)

    @pl.loop(0, 8)
    def _(i):
        norm(pl.multiple_of(EDGE + i * 32, 16), 32)

    first_c.wait_recv()
    mirrors_c = [send(weights.at[2, :, xo(-s), z, y], sibling)]
    pl.when(c == 0)(far_c.wait_recv)
    mirror_far_c = send(weights.at[2, :, xo(2), z, y], sibling, c == 0)
    mirrors = [[], []]
    for i, k in enumerate((1, 2, 3)):
        for third in (0, 1):
            near[2 * i + third].wait_recv()
            mirrors[third].append(send(weights.at[third, :, x, zo(-s * k), y], sibling))
    far.wait_recv()
    mirror_far = send(weights.at[c, :, x, zo(4), y], sibling)

    mirrors_c[0].wait_recv()
    pl.when(c == 1)(mirror_far_c.wait_recv)
    line_c = send(weights.at[2, :, :, z, y], y_dev)
    for third in (0, 1):
        for copy in mirrors[third]:
            copy.wait_recv()
    mirror_far.wait_recv()
    line_a = send(weights.at[0, :, x, :, y], y_dev)
    line_b = send(weights.at[1, :, x, :, y], x_dev)

    @pl.loop(8, 16)
    def _(i):
        norm(pl.multiple_of(EDGE + i * 32, 16), 32)

    hz = pl.ds(pl.multiple_of(4 * c, 4), 4)
    hx = pl.ds(pl.multiple_of(2 * c, 2), 2)
    line_c.wait_recv()
    line2_c = send(weights.at[2, :, hx, z, yo(-s)], y_dev)
    m_c1 = send(weights.at[2, :, :, z, yo(-s)], sibling)
    line_a.wait_recv()
    line2_a = send(weights.at[0, :, x, hz, yo(-s)], y_dev)
    m_a1 = send(weights.at[0, :, x, :, yo(-s)], sibling)
    line_b.wait_recv()
    line2_b = send(weights.at[1, :, xo(-s), hz, y], x_dev)
    m_b1 = send(weights.at[1, :, xo(-s), :, y], sibling)

    for copy in halo:
        copy.wait_recv()
    norm(0, EDGE)
    norm(EDGE + ROWS, EDGE)

    for load in loads[5:]:
        load.wait()
    base = (block * 4) % 8 + 8
    for i in range(6):
        q = base + i - 1
        there = block * 4 + i - 1
        row = seg_raw[pl.ds(q, 1), :].astype(F32)
        row = jnp.where(jnp.logical_or(there < 0, there >= 1024), -1.0, row)
        seg_col[pl.ds(128 * i, 128), :] = jnp.transpose(jnp.broadcast_to(row, (128, 128)))

    @pl.loop(0, 16)
    def _(i):
        r0 = pl.multiple_of(i * 32, 32)
        center = seg_col[pl.ds(r0 + 128, 32), :]
        low = jnp.zeros((32, 128), F32)
        high = jnp.zeros((32, 128), F32)
        for d in range(1, HALF + 1):
            low = low + jnp.where(seg_col[pl.ds(r0 + 128 - d, 32), :] == center, 1.0, 0.0)
            high = high + jnp.where(seg_col[pl.ds(r0 + 128 + d, 32), :] == center, 1.0, 0.0)
        before[pl.ds(r0, 32), :] = low
        after[pl.ds(r0, 32), :] = high

    line2_c.wait_recv()
    m_c2 = send(weights.at[2, :, hx, z, yo(-2 * s)], sibling)
    line2_a.wait_recv()
    m_a2 = send(weights.at[0, :, x, hz, yo(-2 * s)], sibling)
    line2_b.wait_recv()
    m_b2 = send(weights.at[1, :, xo(-2 * s), hz, y], sibling)

    order = (0, -1, 1, 2)

    def a_line(p, px, i):
        return weights.at[0, p, px, :, yo(s * order[i])]

    def a_half(p, px, i):
        return weights.at[0, p, px, hz, yo(s * order[i])]

    def b_line(p, py, i):
        return weights.at[1, p, xo(s * order[i]), :, py]

    def b_half(p, py, i):
        return weights.at[1, p, xo(s * order[i]), hz, py]

    def c_line(p, pz, i):
        return weights.at[2, p, :, pz, yo(s * order[i])]

    def c_half(p, pz, i):
        return weights.at[2, p, hx, pz, yo(s * order[i])]

    st = {}

    def own(p):
        st["a1", p], st["b1", p], st["c1", p] = [], [], []
        for i in range(4):
            if p == 0 and i == 2:
                m_a1.wait_recv()
                m_b1.wait_recv()
                m_c1.wait_recv()
            if p == 0 and i == 3:
                m_a2.wait_recv()
                m_b2.wait_recv()
                m_c2.wait_recv()
            st["c1", p].append(send(c_line(p, z, i), z_dev))
            st["a1", p].append(send(a_line(p, x, i), x_dev))
            st["b1", p].append(send(b_line(p, y, i), y_dev))

    def relay(p, i):
        if i == 0:
            st["a2", p], st["b2", p], st["c2", p] = [], [], []
        st["c1", p][i].wait_recv()
        st["c2", p].append(send(c_line(p, zo(-s), i), z_dev))
        st["a1", p][i].wait_recv()
        st["a2", p].append(send(a_half(p, xo(-s), i), x_dev))
        st["b1", p][i].wait_recv()
        st["b2", p].append(send(b_half(p, yo(-s), i), y_dev))
        if i == 3:
            st["ma1", p] = send(weights.at[0, p, xo(-s)], sibling)
            st["mb1", p] = send(weights.at[1, p, :, :, yo(-s)], sibling)
            st["mc1", p] = send(weights.at[2, p, :, zo(-s)], sibling)

    def c_step(p, k):
        nxt_k = []
        for i in range(4):
            st["c%d" % k, p][i].wait_recv()
            if k == 2:
                nxt_k.append(send(c_line(p, zo(-2 * s), i), z_dev))
            elif k == 3:
                nxt_k.append(send(c_half(p, zo(-3 * s), i), z_dev))
        st["c%d" % (k + 1), p] = nxt_k
        if k < 4:
            st["mc%d" % k, p] = send(weights.at[2, p, :, zo(-k * s)], sibling)
        else:
            st["mc%d" % k, p] = send(weights.at[2, p, hx, zo(4)], sibling)

    def ab_end(p):
        for i in range(4):
            st["a2", p][i].wait_recv()
        st["ma2", p] = send(weights.at[0, p, xo(2), hz], sibling)
        for i in range(4):
            st["b2", p][i].wait_recv()
        st["mb2", p] = send(weights.at[1, p, :, hz, yo(2)], sibling)

    def have_a(p):
        st["ma1", p].wait_recv()
        st["ma2", p].wait_recv()

    def have_b(p):
        st["mb1", p].wait_recv()
        st["mb2", p].wait_recv()

    def have_c(p):
        for k in range(1, 5):
            st["mc%d" % k, p].wait_recv()

    def expand(p, t):
        rhs = jnp.concatenate(
            [weights[t, p, g].reshape(D, 128) for g in (0, 1, 2, 3)], axis=1
        )
        both = jnp.dot(normed[...], rhs, preferred_element_type=F32)
        units = both[:, :256] * sigmoid(both[:, 256:])
        units = units.astype(BF16).astype(F32)
        gated[0] = units[:, :128]
        gated[1] = units[:, 128:]

    def conv(p, t, quarter):
        @pl.loop(4 * quarter, 4 * quarter + 4)
        def _(i):
            r0 = pl.multiple_of(i * 32, 32)
            low = before[pl.ds(r0, 32), :]
            high = after[pl.ds(r0, 32), :]
            sums = [None, None]
            for o in range(TAPS):
                d = o - HALF
                keep = low >= float(-d) if d < 0 else high >= float(d)
                for g in range(2):
                    ch = 768 * g + 128 * (3 * p + t)
                    v = gated[g, pl.ds(r0 + o + 1, 32), :]
                    if d != 0:
                        v = jnp.where(keep, v, 0.0)
                    v = v * taps_v[o : o + 1, ch : ch + 128]
                    sums[g] = v if sums[g] is None else sums[g] + v
            for g in range(2):
                l = 6 * g + 3 * p + t
                ch = 128 * l
                h = sums[g] * scale_v[l : l + 1, :] + shift_v[l : l + 1, :]
                active[pl.ds(r0, 32), ch : ch + 128] = (h * sigmoid(h)).astype(BF16)

    def unit(p, t, events):
        expand(p, t)
        if events:
            events.pop(0)()
        for quarter in range(4):
            conv(p, t, quarter)
            if events:
                events.pop(0)()

    own(0)
    for i in range(4):
        relay(0, i)
    own(1)
    c_step(0, 2)
    ab_end(0)
    have_a(0)
    E = functools.partial
    events = [E(c_step, 0, 3)] + [E(relay, 1, i) for i in range(4)] + [
        E(own, 2), E(c_step, 0, 4), E(c_step, 1, 2), E(ab_end, 1),
    ]
    unit(0, 0, events)
    have_b(0)
    unit(0, 1, events)
    for e in events:
        e()
    have_c(0)
    events = [E(relay, 2, i) for i in range(4)] + [
        E(c_step, 1, 3), E(c_step, 1, 4), E(c_step, 2, 2), E(ab_end, 2), E(c_step, 2, 3), E(c_step, 2, 4)
    ]
    unit(0, 2, events)
    have_a(1)
    unit(1, 0, events)
    have_b(1)
    for e in events:
        e()
    events = []
    unit(1, 1, events)
    have_c(1)
    unit(1, 2, events)
    have_a(2)
    have_b(2)
    have_c(2)
    stores = []
    for g in range(NX):
        rhs = jnp.concatenate([weights[t, 2, g].reshape(D, 128) for t in range(3)], axis=1)
        cols = pl.ds(384 * g, 384)
        product = jnp.dot(active[...], rhs, preferred_element_type=F32)
        result[:, cols] = (product + rows[pl.ds(EDGE, ROWS), cols].astype(F32)).astype(BF16)
        store = pltpu.make_async_copy(result.at[:, cols], out.at[:, cols], local_sem.at[13 + g])
        store.start()
        stores.append(store)
    for copy, when in sent:
        if when is None:
            copy.wait_send()
        else:
            pl.when(when)(copy.wait_send)
    for store in stores:
        store.wait()


def local(frames, segments, norm_gain, norm_bias, expand_weight, conv_kernel, batch_scale, batch_shift, project_weight):
    return pl.pallas_call(
        kernel,
        out_shape=jax.ShapeDtypeStruct((ROWS, D), BF16),
        in_specs=[pl.BlockSpec(memory_space=pltpu.HBM)] * 9,
        out_specs=pl.BlockSpec(memory_space=pltpu.HBM),
        scratch_shapes=[
            pltpu.VMEM((3, 3, NX, NZ, NY, 48, 128), BF16),
            pltpu.VMEM((ALL, D), BF16),
            pltpu.VMEM((ALL, D), BF16),
            pltpu.VMEM((ROWS, D), BF16),
            pltpu.VMEM((ROWS, D), BF16),
            pltpu.VMEM((2, ALL, 128), F32),
            pltpu.VMEM((24, 128), jnp.int32),
            pltpu.VMEM((768, 128), F32),
            pltpu.VMEM((ROWS, 128), F32),
            pltpu.VMEM((ROWS, 128), F32),
            pltpu.VMEM((192, 96), BF16),
            pltpu.VMEM((48, 192), BF16),
            pltpu.VMEM((192, 48), BF16),
            pltpu.VMEM((8, 48, 96), BF16),
            pltpu.VMEM((8, 48, 48), BF16),
            pltpu.VMEM((12, 128), F32),
            pltpu.VMEM((12, 128), F32),
            pltpu.VMEM((TAPS, D), F32),
            pltpu.VMEM((12, 128), F32),
            pltpu.VMEM((12, 128), F32),
            pltpu.SemaphoreType.DMA((20,)),
            pltpu.SemaphoreType.DMA((SEMS,)),
            pltpu.SemaphoreType.DMA((SEMS,)),
        ],
        compiler_params=pltpu.CompilerParams(
            collective_id=0, has_side_effects=True, vmem_limit_bytes=60 << 20
        ),
        name="conformer",
    )(
        frames,
        segments.reshape(1024, 128),
        norm_gain.reshape(12, 128),
        norm_bias.reshape(12, 128),
        expand_weight,
        conv_kernel,
        batch_scale.reshape(12, 128),
        batch_shift.reshape(12, 128),
        project_weight.T,
    )


def solution(mesh):
    in_specs = (
        P(("dp", "fsdp"), None),
        P(),
        P(),
        P(),
        P("fsdp", "dp"),
        P(),
        P(),
        P(),
        P("fsdp", "dp"),
    )
    out_specs = P(("dp", "fsdp"), None)
    return jax.shard_map(local, mesh=mesh, in_specs=in_specs, out_specs=out_specs, check_vma=False)
```

time: 197 us -> 92.1 us (0.47)
  the two profiles are of different devices: /device:TPU:1 before, /device:TPU:2 now
where the time goes in v1:
time: 92.1 us; the launch traced here: 92 us
  Pallas kernels  89.3 us (97%)
  local copies, waits for them, and re-layouts  2.65 us (3%)
    pallas_call x1, Pallas kernels, local(): pl.pallas_call(kernel, out_shape=jax.ShapeDtypeStruct((ROWS, D), BF16), i...  89.3 us
    unnamed x1, local copies, waits for them, and re-layouts  2.65 us

profile of v1, /device:TPU:2, one launch (start us, length us, event | category | flops | bytes accessed | tf_op | source)
XLA Modules:
  0.0 92.0 jit_solution(454521495628278600)
XLA Ops:
  0.0 89.3 %conformer.1 = bf16[512,1536]{1,0:T(8,128)(2,1)} custom-call(bf16[512,1536]{1,0:T(8,128)(2,1)} %frames.1, s32[1024,128]{1,0:T(8,128)} %bitcast.6, f32[12,128]{1,0:T(8,128)} %bitcast.8, f32[12,128]{1,0:T(8,128)} %bitcast.9, bf16[192,96]{1,0:T(8,128)(2,1)} %w1.1, f32[31,1536]{1,0:T(8,128)} %taps.1, f32[12,128]{1,0:T(8,128)} %bitcast.10, f32[12,128]{1,0:T(8,128)} %bitcast.11, ...), custom_call_target="tpu_custom_call" | custom-call | tf_op jit(solution)/shard_map/conformer/pallas_call | solution.py:439
  89.4 2.7 %copy.11 = bf16[512,1536]{1,0:T(8,128)(2,1)} copy(bf16[512,1536]{1,0:T(8,128)(2,1)} %conformer.1) | data formatting | bytes 3145728
